TPU v7x, 256 devices: a whole 4x4x8 slice. The times are simulated.
256 devices in a mesh: ctx: 64 (over x_lo, z, y), head: 4 (over x_hi, core).
Axes of the slice: x: 4 (x_hi: 2, x_lo: 2; x = x_hi * 2 + x_lo), y: 4, z: 8, core: 2. Of those that a mesh axis runs over, the one named last changes fastest.
Arguments:
- queries: bfloat16 [8192, 64, 576], P('ctx', 'head')
- compressed_kv: bfloat16 [8192, 576], P(('ctx', 'head')), may hold values from -4.5 to 4.5
- segment_ids: int32 [8192], P(('ctx', 'head')), may hold values from 0 to 11, never falling along the last dimension, each value on 1 to 2176 neighbouring positions
- value_up: bfloat16 [64, 512, 128], P('head'), may hold values from -0.25 to 0.25
Outputs:
- head_values: bfloat16 [8192, 8192], P('ctx', 'head')
Inputs may be any that keep to these rules, and one draw needn't show every extreme that they name: `segment_ids`: ids never fall along the sequence and every document holds at most 2176 tokens; one holds exactly 2176.
All inputs are finite; a program needn't handle non-finite values.
Results may differ from a plain program's by a relative error of at most 0.0085.
Values may be sent and summed in bfloat16 or wider, within the bound.
A program may use at most 192 MiB of HBM per device.

v0:
```python
import functools
import math

import jax
import jax.numpy as jnp
import numpy as np
from jax import lax
from jax.experimental import pallas as pl
from jax.experimental.pallas import tpu as pltpu
from jax.sharding import PartitionSpec as P

MESH = pl.DeviceIdType.MESH
f32 = jnp.float32
bf16 = jnp.bfloat16

CTX = 64
TOK = 128
HEADS = 16
ROWS = TOK * HEADS
LATENT = 512
ROPE = 64
VDIM = 128
LANES = 128
QTR = TOK // 4
HALF = 2 * QTR
WIDTH = 640
BACK = 18
MASKED = -(2.0**100)
LOG_SCALE = (192.0**-0.5) * math.log2(math.e)
TILE = 512
GROUPS = ((0, 2), (2, 2), (4, 4), (8, 4), (12, 4), (16, 2))
QUARTERS_SENT = 35


def rope_table():
    freq = np.float32(10000.0) ** (-np.arange(ROPE // 2, dtype=np.float32) / np.float32(ROPE // 2))
    angle = (np.arange(CTX * TOK, dtype=np.float32)[:, None] * freq[None, :]).astype(np.float64)
    cos, sin = np.cos(angle), np.sin(angle)
    return np.concatenate([cos, cos, -sin, sin], axis=1).astype(np.float32)


def swap_halves(x):
    half = x.shape[-1] // 2
    return jnp.concatenate([x[..., half:], x[..., :half]], axis=-1)


def kernel(
    table_hbm, q_hbm, kv_ref, seg_ref, up_hbm, out_hbm,
    keys, q, q_rope, table, acc, top, total, s0, s1, p0, p1, f0, f1, up, out,
    in_sem, out_sem, send_sem, core_send_sem, z_sem, x_sem, row_sem, core_sem,
):
    c = lax.axis_index("ctx")
    h = lax.axis_index("head")
    x_hi, core = h // 2, h % 2
    y = c % 4
    mate_x = (1 - x_hi) * 2 + core
    mate_core = x_hi * 2 + (1 - core)
    quarter = pl.ds(pl.multiple_of(core * HALF + x_hi * QTR, QTR), QTR)
    half = pl.ds(pl.multiple_of(core * HALF, HALF), HALF)

    def ctx(by):
        return lax.rem(c + by + CTX, CTX)

    table_in = pltpu.make_async_copy(
        table_hbm.at[pl.ds(pl.multiple_of(c * TOK, TOK), TOK)], table, in_sem.at[0]
    )
    table_in.start()
    q_in = pltpu.make_async_copy(q_hbm.at[:, pl.ds(0, LATENT)], q.at[:, pl.ds(0, LATENT)], in_sem.at[1])
    q_rope_in = pltpu.make_async_copy(q_hbm.at[:, pl.ds(LATENT, ROPE)], q_rope, in_sem.at[2])
    q_rope_in.start()
    q_in.start()
    up_in = pltpu.make_async_copy(up_hbm, up, in_sem.at[3])

    barrier = pltpu.get_barrier_semaphore()

    def greet(to_ctx, to_head):
        pl.semaphore_signal(barrier, inc=1, device_id=(to_ctx, to_head), device_id_type=MESH)

    greet(c, mate_core)
    greet(c, mate_x)
    for k in range(1, 5):
        greet(ctx(-4 * k), h)
    row = 4 * (c // 4)
    for other in (core, 2 + core):
        greet(ctx(-1), other)
        for e in range(1, 4):
            greet(row + lax.rem(y - e + 4, 4), other)

    table_in.wait()
    own_rope = kv_ref[:, LATENT:].astype(f32)
    own_table = table[pl.ds(pl.multiple_of(h * QTR, QTR), QTR), :]
    own_rope = own_rope * own_table[:, :ROPE] + swap_halves(own_rope) * own_table[:, ROPE:]
    place = lax.broadcasted_iota(jnp.int32, (QTR, ROPE), 0)
    ids = jnp.zeros((QTR, ROPE), jnp.int32)
    for j in range(QTR):
        ids = jnp.where(place == j, seg_ref[j], ids)
    own_mark = jnp.where(lax.broadcasted_iota(jnp.int32, (QTR, ROPE), 1) == ids, 1.0, 0.0)
    keys[0, quarter, :LATENT] = kv_ref[:, :LATENT]
    keys[0, quarter, LATENT:] = jnp.concatenate([own_rope, own_mark], axis=1).astype(bf16)

    pl.semaphore_wait(barrier, 14)

    def send(k, d, to_ctx, to_head, sem):
        pltpu.make_async_remote_copy(
            src_ref=keys.at[4 * k, quarter],
            dst_ref=keys.at[d, quarter],
            send_sem=send_sem.at[0],
            recv_sem=sem,
            device_id=(to_ctx, to_head),
            device_id_type=MESH,
        ).start()

    def to_row(k, e, g, to_ctx):
        for other in (core, 2 + core):
            send(k, 4 * g + e, to_ctx, other, row_sem.at[4 * g + e])

    def pass_on(k):
        if k:
            pltpu.make_async_copy(keys.at[4 * k, quarter], keys.at[4 * k, quarter], z_sem.at[k]).wait()
        send(k, 4 * k, c, mate_x, x_sem.at[k])
        for e in (1, 3, 2):
            wrap = jnp.where(y + e >= 4, 1, 0)
            there = ctx(e - 4 * wrap)
            if e == 1 and k in (0, 4):
                to_row(k, e, k, ctx(1))
            if k == 0 and e > 1 or k == 1 and e == 1:
                pl.when(wrap == 0)(functools.partial(to_row, k, e, k, there))
            elif k == 4:
                pl.when(wrap == 1)(functools.partial(to_row, k, e, k - 1, there))
            elif k:
                to_row(k, e, k - wrap, there)

    def send_column(k):
        send(0, 4 * k, ctx(4 * k), h, z_sem.at[k])

    send_column(1)
    pass_on(0)
    for k in range(2, 5):
        send_column(k)
    up_in.start()

    def share(group):
        first, count = GROUPS[group]
        for d in range(first, first + count):
            if d % 4 == 0:
                pltpu.make_async_copy(keys.at[d, quarter], keys.at[d, quarter], x_sem.at[d // 4]).wait()
            else:
                pltpu.make_async_copy(keys.at[d, half], keys.at[d, half], row_sem.at[d]).wait()
        mine = keys.at[pl.ds(first, count), half]
        pltpu.make_async_remote_copy(
            src_ref=mine,
            dst_ref=mine,
            send_sem=core_send_sem.at[0],
            recv_sem=core_sem.at[group],
            device_id=(c, mate_core),
            device_id_type=MESH,
        ).start()

    def shared(group):
        first, count = GROUPS[group]
        theirs = keys.at[pl.ds(first, count), half]
        pltpu.make_async_copy(theirs, theirs, core_sem.at[group]).wait()

    q_rope_in.wait()
    for t in range(0, TOK, 32):
        part = q_rope[t * HEADS : (t + 32) * HEADS, :].astype(f32).reshape(32, HEADS, ROPE)
        cos = table[t : t + 32, :ROPE][:, None, :]
        sin = table[t : t + 32, ROPE:][:, None, :]
        part = part * cos + swap_halves(part) * sin
        q[t * HEADS : (t + 32) * HEADS, LATENT : LATENT + ROPE] = part.reshape(32 * HEADS, ROPE).astype(bf16)

    share(0)
    pass_on(1)
    q_in.wait()
    shared(0)

    for j in range(4):
        at = (j % 2) * HALF + (j // 2) * QTR
        mark = (keys[0, at : at + QTR, LATENT + ROPE :].astype(f32) - 1.0) * (-MASKED)
        mark = jnp.broadcast_to(mark[:, None, :], (QTR, HEADS, ROPE)).reshape(QTR * HEADS, ROPE)
        q[j * QTR * HEADS : (j + 1) * QTR * HEADS, LATENT + ROPE :] = mark.astype(bf16)

    tiles = ROWS // TILE
    work = [(g, t) for g in range(len(GROUPS)) for t in range(tiles)]
    scores, weights, factors = (s0, s1), (p0, p1), (f0, f1)

    def group_keys(group, columns):
        first, count = GROUPS[group]
        return keys[first : first + count, :, :columns].reshape(count * TOK, columns)

    def score(i):
        group, t = work[i]
        size = GROUPS[group][1] * TOK
        scores[i % 2][:, :size] = lax.dot_general(
            q[t * TILE : (t + 1) * TILE, :],
            group_keys(group, WIDTH),
            (((1,), (1,)), ((), ())),
            preferred_element_type=f32,
        )

    def weigh(i):
        group, t = work[i]
        count = GROUPS[group][1]
        at = slice(t * TILE, (t + 1) * TILE)
        parts = [scores[i % 2][:, j * TOK : (j + 1) * TOK] for j in range(count)]
        if group == 0:
            lane = lax.broadcasted_iota(jnp.int32, (TILE, TOK), 1)
            key_at = (lane // QTR % 2) * HALF + (lane // HALF) * QTR + lane % QTR
            query_at = lax.broadcasted_iota(jnp.int32, (TILE, TOK), 0) // HEADS + t * (TILE // HEADS)
            parts[0] = jnp.where(key_at <= query_at, parts[0], MASKED)
        high = functools.reduce(jnp.maximum, parts)
        high = jnp.max(high, axis=1, keepdims=True)
        if group == 0:
            high = jnp.broadcast_to(high, (TILE, TOK))
        else:
            before = top[at, :]
            high = jnp.maximum(before, high)
        shift = high * LOG_SCALE
        added = None
        for j in range(count):
            raw = jnp.exp2(parts[j] * LOG_SCALE - shift)
            weights[i % 2][:, j * TOK : (j + 1) * TOK] = raw.astype(bf16)
            added = raw if added is None else added + raw
        top[at, :] = high
        if group == 0:
            total[at, :] = added
        else:
            factor = jnp.exp2(before * LOG_SCALE - shift)
            factors[i % 2][...] = factor
            total[at, :] = total[at, :] * factor + added

    def mix(i):
        group, t = work[i]
        at = slice(t * TILE, (t + 1) * TILE)
        size = GROUPS[group][1] * TOK
        mixed = jnp.dot(weights[i % 2][:, :size], group_keys(group, LATENT), preferred_element_type=f32)
        for j in range(LATENT // LANES):
            part = mixed[:, j * LANES : (j + 1) * LANES]
            if group == 0:
                acc[j, at, :] = part
            else:
                acc[j, at, :] = acc[j, at, :] * factors[i % 2][...] + part

    before_step = {
        0: [lambda: pass_on(2)],
        1: [lambda: share(1)],
        2: [lambda: shared(1), lambda: pass_on(3)],
        5: [lambda: share(2)],
        6: [lambda: shared(2), lambda: pass_on(4)],
        9: [lambda: share(3)],
        10: [lambda: shared(3)],
        13: [lambda: share(4)],
        14: [lambda: shared(4)],
        17: [lambda: share(5)],
        18: [lambda: shared(5)],
    }
    score(0)
    score(1)
    weigh(0)
    for i in range(len(work)):
        for event in before_step.get(i, ()):
            event()
        mix(i)
        if i + 1 < len(work):
            weigh(i + 1)
        if i + 2 < len(work):
            score(i + 2)

    up_in.wait()
    per_copy = 4
    copies = []
    for head in range(HEADS):
        rows = pl.ds(head, TOK, stride=HEADS)
        share_of = 1.0 / jnp.sum(total[rows, :], axis=1, keepdims=True)
        mixed_latent = jnp.concatenate(
            [(acc[j, rows, :] * share_of).astype(bf16) for j in range(LATENT // LANES)], axis=1
        )
        out[:, head * VDIM : (head + 1) * VDIM] = jnp.dot(
            mixed_latent, up[head], preferred_element_type=f32
        ).astype(bf16)
        if head % per_copy == per_copy - 1:
            done = pl.ds((head + 1 - per_copy) * VDIM, per_copy * VDIM)
            copies.append(pltpu.make_async_copy(out.at[:, done], out_hbm.at[:, done], out_sem.at[head // per_copy]))
            copies[-1].start()
    everything = q.at[pl.ds(0, QUARTERS_SENT * QTR)]
    pltpu.make_async_copy(everything, everything, send_sem.at[0]).wait()
    everything = q.at[pl.ds(0, BACK * HALF)]
    pltpu.make_async_copy(everything, everything, core_send_sem.at[0]).wait()
    for copy in copies:
        copy.wait()


def local(queries, compressed_kv, segment_ids, value_up):
    any_space = pl.BlockSpec(memory_space=pl.ANY)
    return pl.pallas_call(
        kernel,
        out_shape=jax.ShapeDtypeStruct((TOK, HEADS * VDIM), bf16),
        in_specs=[
            any_space,
            any_space,
            pl.BlockSpec(memory_space=pltpu.VMEM),
            pl.BlockSpec(memory_space=pltpu.SMEM),
            any_space,
        ],
        out_specs=any_space,
        scratch_shapes=[
            pltpu.VMEM((BACK, TOK, WIDTH), bf16),
            pltpu.VMEM((ROWS, WIDTH), bf16),
            pltpu.VMEM((ROWS, ROPE), bf16),
            pltpu.VMEM((TOK, 2 * ROPE), f32),
            pltpu.VMEM((LATENT // LANES, ROWS, LANES), f32),
            pltpu.VMEM((ROWS, TOK), f32),
            pltpu.VMEM((ROWS, TOK), f32),
            pltpu.VMEM((TILE, 4 * TOK), f32),
            pltpu.VMEM((TILE, 4 * TOK), f32),
            pltpu.VMEM((TILE, 4 * TOK), bf16),
            pltpu.VMEM((TILE, 4 * TOK), bf16),
            pltpu.VMEM((TILE, TOK), f32),
            pltpu.VMEM((TILE, TOK), f32),
            pltpu.VMEM((HEADS, LATENT, VDIM), bf16),
            pltpu.VMEM((TOK, HEADS * VDIM), bf16),
            pltpu.SemaphoreType.DMA((4,)),
            pltpu.SemaphoreType.DMA((4,)),
            pltpu.SemaphoreType.DMA((1,)),
            pltpu.SemaphoreType.DMA((1,)),
            pltpu.SemaphoreType.DMA((5,)),
            pltpu.SemaphoreType.DMA((5,)),
            pltpu.SemaphoreType.DMA((BACK,)),
            pltpu.SemaphoreType.DMA((len(GROUPS),)),
        ],
        compiler_params=pltpu.CompilerParams(
            collective_id=0, has_side_effects=True, vmem_limit_bytes=44 << 20
        ),
        name="latent_attention",
    )(
        jnp.asarray(rope_table()),
        queries.reshape(ROWS, LATENT + ROPE),
        compressed_kv,
        segment_ids,
        value_up,
    )


def solution(mesh):
    in_specs = (
        P("ctx", "head", None),
        P(("ctx", "head"), None),
        P(("ctx", "head")),
        P("head", None, None),
    )
    return jax.shard_map(
        local, mesh=mesh, in_specs=in_specs, out_specs=P("ctx", "head"), check_vma=False
    )
```

profile of v0, /device:TPU:1, one launch (start us, length us, event | category | flops | bytes accessed | tf_op | source)
XLA Modules:
  0.0 59.2 jit_solution(8397656435665396731)
XLA Ops:
  0.0 0.0 copy-start.3
  0.0 0.0 copy-start.2
  0.0 3.9 %copy.6 = bf16[128,16,576]{2,1,0:T(8,128)(2,1)S(1)} copy(bf16[128,16,576]{0,2,1:T(8,128)(2,1)} %param.5) | data formatting | bytes 4718592 | tf_op args[0]
  3.9 0.0 copy-done.3
  4.0 0.0 copy-done.2
  4.0 0.0 copy-start
  4.0 2.2 %copy-done = f32[8192,128]{1,0:T(8,128)S(1)} copy-done((f32[8192,128]{1,0:T(8,128)S(1)}, f32[8192,128]{1,0:T(8,128)}, u32[]{:S(2)}) %copy-start) | copy-done | bytes 4194328
  6.2 0.0 copy-start.1
  6.2 1.6 %copy-done.1 = bf16[16,512,128]{2,1,0:T(8,128)(2,1)S(1)} copy-done((bf16[16,512,128]{2,1,0:T(8,128)(2,1)S(1)}, bf16[16,512,128]{2,1,0:T(8,128)(2,1)}, u32[]{:S(2)}) %copy-start.1) | copy-done | bytes 2097176
  7.8 50.6 %latent_attention.1 = bf16[128,2048]{1,0:T(8,128)(2,1)S(1)} custom-call(f32[8192,128]{1,0:T(8,128)S(1)} %copy-done, bf16[2048,576]{1,0:T(8,128)(2,1)S(1)} %bitcast.1, bf16[32,576]{1,0:T(8,128)(2,1)S(1)} %copy-done.2, s32[32]{0:T(128)S(1)} %copy-done.3, bf16[16,512,128]{2,1,0:T(8,128)(2,1)S(1)} %copy-done.1), custom_call_target="tpu_custom_call" | custom-call | tf_op jit(solution)/shard_map/latent_attention/pallas_call | solution.py:295
  58.4 0.8 %copy.8 = bf16[128,2048]{1,0:T(8,128)(2,1)} copy(bf16[128,2048]{1,0:T(8,128)(2,1)S(1)} %latent_attention.1) | data formatting | bytes 1048576
Async XLA Ops:
  0.0 4.0 %copy-start.3 = (s32[32]{0:T(128)S(1)}, s32[32]{0:T(128)}, u32[]{:S(2)}) copy-start(s32[32]{0:T(128)} %seg_ref.1) | copy-start | bytes 388
  0.0 4.0 %copy-start.2 = (bf16[32,576]{1,0:T(8,128)(2,1)S(1)}, bf16[32,576]{1,0:T(8,128)(2,1)}, u32[]{:S(2)}) copy-start(bf16[32,576]{1,0:T(8,128)(2,1)} %kv_ref.1) | copy-start | bytes 110596
  4.0 2.2 %copy-start = (f32[8192,128]{1,0:T(8,128)S(1)}, f32[8192,128]{1,0:T(8,128)}, u32[]{:S(2)}) copy-start(f32[8192,128]{1,0:T(8,128)} %constant.2.clone.table_hbm) | copy-start | bytes 12582916
  6.2 1.6 %copy-start.1 = (bf16[16,512,128]{2,1,0:T(8,128)(2,1)S(1)}, bf16[16,512,128]{2,1,0:T(8,128)(2,1)}, u32[]{:S(2)}) copy-start(bf16[16,512,128]{2,1,0:T(8,128)(2,1)} %up_hbm.1) | copy-start | bytes 6291460
where the time goes:
time: 59.3 us; the launch traced here: 59.2 us
  Pallas kernels  50.6 us (85%)
  local copies, waits for them, and re-layouts  8.51 us (14%)
    pallas_call x1, Pallas kernels, local(): pl.pallas_call(kernel, out_shape=jax.ShapeDtypeStruct((TOK, HEADS * VDIM)...  50.6 us
    unnamed x10, local copies, waits for them, and re-layouts  8.51 us

commit v1 on v0

v1 whole, which is shorter than its diff:
```python
import functools
import math

import jax
import jax.numpy as jnp
import numpy as np
from jax import lax
from jax.experimental import pallas as pl
from jax.experimental.pallas import tpu as pltpu
from jax.sharding import PartitionSpec as P

MESH = pl.DeviceIdType.MESH
f32 = jnp.float32
bf16 = jnp.bfloat16

CTX = 64
TOK = 128
HEADS = 16
ROWS = TOK * HEADS
LATENT = 512
ROPE = 64
VDIM = 128
LANES = 128
QTR = TOK // 4
HALF = 2 * QTR
WIDTH = 640
BACK = 18
MASKED = -(2.0**100)
LOG_SCALE = (192.0**-0.5) * math.log2(math.e)
TILE = 512
GROUPS = ((0, 2), (2, 2), (4, 4), (8, 4), (12, 4), (16, 2))
HALF_ROPE = ROPE // 2
SENDS = 57
BY_MATE = ()
FROM_BOTH = (0, 1, 2, 3, 4)


def rope_table():
    freq = np.float32(10000.0) ** (-np.arange(HALF_ROPE, dtype=np.float32) / np.float32(HALF_ROPE))
    position = np.arange(CTX * TOK, dtype=np.float32).reshape(CTX, 1, TOK)
    angle = (position * freq[None, :, None]).astype(np.float64)
    return np.concatenate([np.cos(angle), np.sin(angle)], axis=1).astype(np.float32)


def kernel(
    table_hbm, q_hbm, kv_hbm, seg_hbm, up_hbm, out_hbm,
    keys, q, q_flat, kv, seg, table, table_rows, acc, top, total, s0, s1, p0, p1, f0, f1, up, out,
    in_sem, out_sem, send_sem, core_send_sem, z_sem, x_sem, row_sem, core_sem,
):
    c = lax.axis_index("ctx")
    h = lax.axis_index("head")
    x_hi, core = h // 2, h % 2
    y = c % 4
    mate_x = (1 - x_hi) * 2 + core
    mate_core = x_hi * 2 + (1 - core)
    quarter = pl.ds(pl.multiple_of(core * HALF + x_hi * QTR, QTR), QTR)
    half = pl.ds(pl.multiple_of(core * HALF, HALF), HALF)

    kv_in = pltpu.make_async_copy(kv_hbm, kv, in_sem.at[0])
    seg_in = pltpu.make_async_copy(seg_hbm, seg, in_sem.at[1])
    table_in = pltpu.make_async_copy(table_hbm.at[c], table, in_sem.at[2])
    q_in = pltpu.make_async_copy(q_hbm, q_flat, in_sem.at[3])
    up_in = pltpu.make_async_copy(up_hbm, up, in_sem.at[4])
    for copy in (kv_in, seg_in, table_in, q_in):
        copy.start()

    barrier = pltpu.get_barrier_semaphore()

    def greet(to_ctx, to_head):
        pl.semaphore_signal(barrier, inc=1, device_id=(to_ctx, to_head), device_id_type=MESH)

    row = c - y
    greet(c, mate_core)
    greet(c, mate_x)
    for other in (core, 2 + core):
        for e in range(1, 4):
            greet(row + lax.rem(y - e + 4, 4), other)
        pl.when(c >= 1)(functools.partial(greet, c - 1, other))
    for k in (1, 2):
        pl.when(c >= 4 * k)(functools.partial(greet, c - 4 * k, h))
    expected = 8 + 2 * jnp.where(c + 1 < CTX, 1, 0) + jnp.where(c + 4 < CTX, 1, 0) + jnp.where(c + 8 < CTX, 1, 0)

    @pl.when(c < BACK - 1)
    def _():
        for d in range(1, BACK):

            @pl.when(d > c)
            def _():
                keys[d, half, :LATENT] = jnp.zeros((HALF, LATENT), bf16)
                lane = lax.broadcasted_iota(jnp.int32, (HALF, LANES), 1)
                keys[d, half, LATENT:] = jnp.where(lane < ROPE, 0.0, 1.0).astype(bf16)

    table_in.wait()
    table_rows[...] = table[...].T
    kv_in.wait()
    own_table = table_rows[pl.ds(pl.multiple_of(h * QTR, QTR), QTR), :]
    own_cos, own_sin = own_table[:, :HALF_ROPE], own_table[:, HALF_ROPE:]
    own_rope = kv[:, LATENT:].astype(f32)
    low, high = own_rope[:, :HALF_ROPE], own_rope[:, HALF_ROPE:]
    seg_in.wait()
    place = lax.broadcasted_iota(jnp.int32, (QTR, ROPE), 0)
    ids = jnp.zeros((QTR, ROPE), jnp.int32)
    for j in range(QTR):
        ids = jnp.where(place == j, seg[j], ids)
    own_mark = jnp.where(lax.broadcasted_iota(jnp.int32, (QTR, ROPE), 1) == ids, 1.0, 0.0)
    keys[0, quarter, :LATENT] = kv[:, :LATENT]
    keys[0, quarter, LATENT:] = jnp.concatenate(
        [low * own_cos - high * own_sin, low * own_sin + high * own_cos, own_mark], axis=1
    ).astype(bf16)

    pl.semaphore_wait(barrier, expected)

    sent = []

    def send(src, dst, to_ctx, to_head, sem, when):
        copy = pltpu.make_async_remote_copy(
            src_ref=src,
            dst_ref=dst,
            send_sem=send_sem.at[len(sent)],
            recv_sem=sem,
            device_id=(to_ctx, to_head),
            device_id_type=MESH,
        )
        sent.append((when, copy))
        pl.when(when)(copy.start)

    def arrived(view, sem, when):
        pl.when(when)(pltpu.make_async_copy(view, view, sem).wait)

    def column(k, hops):
        to = c + 4 * hops
        there = keys.at[4 * (k + hops), quarter]
        send(keys.at[4 * k, quarter], there, to, h, z_sem.at[k + hops], (c >= 4 * k) & (to < CTX))

    def across(d):
        send(keys.at[d, quarter], keys.at[d, quarter], c, mate_x, x_sem.at[d], c >= d)

    def relay(k, whole):
        for wrapped in (1, 0):
            for e in (1, 2, 3):
                d = 4 * (k - wrapped) + e
                to = c + e - 4 * wrapped
                if d < 0 or d >= BACK or (d == 1 and wrapped) or whole == (d in BY_MATE or k in FROM_BOTH):
                    continue
                when = (y + e >= 4) == (wrapped == 1)
                if d in (1, 17):
                    when = to < CTX
                when = when & (c >= 4 * k)
                if d in BY_MATE:
                    send(keys.at[4 * k, quarter], keys.at[d, quarter], to, h, row_sem.at[d], when)
                elif whole:
                    send(keys.at[4 * k, half], keys.at[d, half], to, h, row_sem.at[d], when)
                else:
                    for other in (core, 2 + core):
                        send(keys.at[4 * k, quarter], keys.at[d, quarter], to, other, row_sem.at[d], when)

    def column_in(k):
        if k == 0:
            column(0, 1)
            column(0, 2)
        else:
            arrived(keys.at[4 * k, quarter], z_sem.at[k], c >= 4 * k)
        if k == 2:
            column(2, 1)
            column(2, 2)
        across(4 * k)
        relay(k, False)

    def column_whole(k):
        arrived(keys.at[4 * k, quarter], x_sem.at[4 * k], c >= 4 * k)
        relay(k, True)

    def row_in(d):
        arrived(keys.at[d, quarter], row_sem.at[d], c >= d)
        across(d)

    def share(group):
        first, count = GROUPS[group]
        for d in range(first, first + count):
            if d in BY_MATE:
                arrived(keys.at[d, quarter], x_sem.at[d], c >= d)
            elif d % 4:
                arrived(keys.at[d, half], row_sem.at[d], c >= d)
        mine = keys.at[pl.ds(first, count), half]
        pltpu.make_async_remote_copy(
            src_ref=mine,
            dst_ref=mine,
            send_sem=core_send_sem.at[0],
            recv_sem=core_sem.at[group],
            device_id=(c, mate_core),
            device_id_type=MESH,
        ).start()

    def shared(group):
        first, count = GROUPS[group]
        theirs = keys.at[pl.ds(first, count), half]
        pltpu.make_async_copy(theirs, theirs, core_sem.at[group]).wait()

    column_in(0)
    up_in.start()

    q_in.wait()
    cos, sin = table[:HALF_ROPE, :], table[HALF_ROPE:, :]
    for head in range(HEADS):
        at = slice(head * TOK, (head + 1) * TOK)
        for j in range(LATENT // LANES):
            q[at, j * LANES : (j + 1) * LANES] = q_flat[head, j * LANES : (j + 1) * LANES, :].T
        low = q_flat[head, LATENT : LATENT + HALF_ROPE, :].astype(f32)
        high = q_flat[head, LATENT + HALF_ROPE :, :].astype(f32)
        turned = jnp.concatenate([low * cos - high * sin, low * sin + high * cos], axis=0)
        q[at, LATENT : LATENT + ROPE] = turned.T.astype(bf16)

    column_in(1)
    column_whole(0)
    share(0)
    column_in(2)
    shared(0)

    for j in range(4):
        at = (j % 2) * HALF + (j // 2) * QTR
        mark = ((keys[0, at : at + QTR, LATENT + ROPE :].astype(f32) - 1.0) * (-MASKED)).astype(bf16)
        for head in range(HEADS):
            q[head * TOK + j * QTR : head * TOK + (j + 1) * QTR, LATENT + ROPE :] = mark

    tiles = ROWS // TILE
    work = [(g, t) for g in range(len(GROUPS)) for t in range(tiles)]
    scores, weights, factors = (s0, s1), (p0, p1), (f0, f1)

    def group_keys(group, columns):
        first, count = GROUPS[group]
        return keys[first : first + count, :, :columns].reshape(count * TOK, columns)

    def score(i):
        group, t = work[i]
        size = GROUPS[group][1] * TOK
        scores[i % 2][:, :size] = lax.dot_general(
            q[t * TILE : (t + 1) * TILE, :],
            group_keys(group, WIDTH),
            (((1,), (1,)), ((), ())),
            preferred_element_type=f32,
        )

    def weigh(i):
        group, t = work[i]
        count = GROUPS[group][1]
        at = slice(t * TILE, (t + 1) * TILE)
        parts = [scores[i % 2][:, j * TOK : (j + 1) * TOK] for j in range(count)]
        if group == 0:
            lane = lax.broadcasted_iota(jnp.int32, (TILE, TOK), 1)
            key_at = (lane // QTR % 2) * HALF + (lane // HALF) * QTR + lane % QTR
            query_at = lax.broadcasted_iota(jnp.int32, (TILE, TOK), 0) % TOK
            parts[0] = jnp.where(key_at <= query_at, parts[0], MASKED)
        high = functools.reduce(jnp.maximum, parts)
        high = jnp.max(high, axis=1, keepdims=True)
        if group == 0:
            high = jnp.broadcast_to(high, (TILE, TOK))
        else:
            before = top[at, :]
            high = jnp.maximum(before, high)
        shift = high * LOG_SCALE
        added = None
        for j in range(count):
            raw = jnp.exp2(parts[j] * LOG_SCALE - shift)
            weights[i % 2][:, j * TOK : (j + 1) * TOK] = raw.astype(bf16)
            added = raw if added is None else added + raw
        top[at, :] = high
        if group == 0:
            total[at, :] = added
        else:
            factor = jnp.exp2(before * LOG_SCALE - shift)
            factors[i % 2][...] = factor
            total[at, :] = total[at, :] * factor + added

    def mix(i):
        group, t = work[i]
        at = slice(t * TILE, (t + 1) * TILE)
        size = GROUPS[group][1] * TOK
        mixed = jnp.dot(weights[i % 2][:, :size], group_keys(group, LATENT), preferred_element_type=f32)
        if group == 0:
            acc[at, :] = mixed
        else:
            factor = factors[i % 2][...]
            acc[at, :] = acc[at, :] * jnp.concatenate([factor] * (LATENT // LANES), axis=1) + mixed

    copies = []

    def finish(t):
        for head in range(t * TILE // TOK, (t + 1) * TILE // TOK):
            at = slice(head * TOK, (head + 1) * TOK)
            scale = 1.0 / jnp.sum(total[at, :], axis=1, keepdims=True)
            out[:, head * VDIM : (head + 1) * VDIM] = jnp.dot(
                (acc[at, :] * scale).astype(bf16), up[head], preferred_element_type=f32
            ).astype(bf16)
        done = pl.ds(t * TILE, TILE)
        copies.append(pltpu.make_async_copy(out.at[:, done], out_hbm.at[:, done], out_sem.at[t]))
        copies[-1].start()

    before_step = {
        0: [lambda: column_in(3)],
        1: [lambda: column_whole(1), lambda: share(1)],
        2: [lambda: column_in(4), lambda: shared(1)],
        4: [lambda: share(2)],
        6: [lambda: shared(2)],
        8: [lambda: column_whole(2), lambda: share(3)],
        10: [lambda: shared(3)],
        12: [lambda: column_whole(3), lambda: share(4)],
        14: [lambda: shared(4)],
        16: [lambda: column_whole(4), lambda: share(5)],
        18: [lambda: shared(5)],
    }
    score(0)
    score(1)
    weigh(0)
    for i in range(len(work)):
        for event in before_step.get(i, ()):
            event()
        if i == len(work) - tiles:
            up_in.wait()
        mix(i)
        if i + 1 < len(work):
            weigh(i + 1)
        if i + 2 < len(work):
            score(i + 2)
        if i >= len(work) - tiles:
            finish(i - (len(work) - tiles))

    assert len(sent) == SENDS, len(sent)
    for when, copy in sent:
        pl.when(when)(copy.wait_send)
    everything = q.at[pl.ds(0, BACK * HALF)]
    pltpu.make_async_copy(everything, everything, core_send_sem.at[0]).wait()
    for copy in copies:
        copy.wait()


def local(queries, compressed_kv, segment_ids, value_up):
    any_space = pl.BlockSpec(memory_space=pl.ANY)
    return pl.pallas_call(
        kernel,
        out_shape=jax.ShapeDtypeStruct((TOK, HEADS * VDIM), bf16),
        in_specs=[any_space] * 5,
        out_specs=any_space,
        scratch_shapes=[
            pltpu.VMEM((BACK, TOK, WIDTH), bf16),
            pltpu.VMEM((ROWS, WIDTH), bf16),
            pltpu.VMEM((HEADS, LATENT + ROPE, TOK), bf16),
            pltpu.VMEM((QTR, LATENT + ROPE), bf16),
            pltpu.SMEM((QTR,), jnp.int32),
            pltpu.VMEM((ROPE, TOK), f32),
            pltpu.VMEM((TOK, ROPE), f32),
            pltpu.VMEM((ROWS, LATENT), f32),
            pltpu.VMEM((ROWS, TOK), f32),
            pltpu.VMEM((ROWS, TOK), f32),
            pltpu.VMEM((TILE, 4 * TOK), f32),
            pltpu.VMEM((TILE, 4 * TOK), f32),
            pltpu.VMEM((TILE, 4 * TOK), bf16),
            pltpu.VMEM((TILE, 4 * TOK), bf16),
            pltpu.VMEM((TILE, TOK), f32),
            pltpu.VMEM((TILE, TOK), f32),
            pltpu.VMEM((HEADS, LATENT, VDIM), bf16),
            pltpu.VMEM((TOK, HEADS * VDIM), bf16),
            pltpu.SemaphoreType.DMA((5,)),
            pltpu.SemaphoreType.DMA((4,)),
            pltpu.SemaphoreType.DMA((SENDS,)),
            pltpu.SemaphoreType.DMA((1,)),
            pltpu.SemaphoreType.DMA((5,)),
            pltpu.SemaphoreType.DMA((BACK,)),
            pltpu.SemaphoreType.DMA((BACK,)),
            pltpu.SemaphoreType.DMA((len(GROUPS),)),
        ],
        compiler_params=pltpu.CompilerParams(
            collective_id=0, has_side_effects=True, vmem_limit_bytes=62 << 20
        ),
        name="latent_attention",
    )(
        jnp.asarray(rope_table()),
        jnp.transpose(queries, (1, 2, 0)),
        compressed_kv,
        segment_ids,
        value_up,
    )


def solution(mesh):
    in_specs = (
        P("ctx", "head", None),
        P(("ctx", "head"), None),
        P(("ctx", "head")),
        P("head", None, None),
    )
    return jax.shard_map(
        local, mesh=mesh, in_specs=in_specs, out_specs=P("ctx", "head"), check_vma=False
    )
```

time: 59.3 us -> 45 us (0.76)
  the two profiles are of different devices: /device:TPU:1 before, /device:TPU:35 now
where the time goes in v1:
time: 45 us; the launch traced here: 44.9 us
  Pallas kernels  43 us (96%)
  local copies, waits for them, and re-layouts  1.88 us (4%)
    pallas_call x1, Pallas kernels, local(): pl.pallas_call(kernel, out_shape=jax.ShapeDtypeStruct((TOK, HEADS * VDIM)...  43 us
    unnamed x1, local copies, waits for them, and re-layouts  1.88 us

profile of v1, /device:TPU:35, one launch (start us, length us, event | category | flops | bytes accessed | tf_op | source)
XLA Modules:
  0.0 44.9 jit_solution(16931431987307203886)
XLA Ops:
  0.0 43.0 %latent_attention.1 = bf16[128,2048]{1,0:T(8,128)(2,1)} custom-call(f32[64,64,128]{2,1,0:T(8,128)} %constant.2.clone.table_hbm, bf16[16,576,128]{2,1,0:T(8,128)(2,1)} %bitcast.1, bf16[32,576]{1,0:T(8,128)(2,1)} %kv_hbm.1, s32[32]{0:T(128)} %seg_hbm.1, bf16[16,512,128]{2,1,0:T(8,128)(2,1)} %up_hbm.1), custom_call_target="tpu_custom_call" | custom-call | tf_op jit(solution)/shard_map/latent_attention/pallas_call | solution.py:338
  43.0 1.9 %copy.7 = bf16[128,2048]{1,0:T(8,128)(2,1)} copy(bf16[128,2048]{1,0:T(8,128)(2,1)} %latent_attention.1) | data formatting | bytes 1048576

commit v2 on v1

--- a/solution.py
+++ b/solution.py
@@ -90,20 +90,20 @@
                 lane = lax.broadcasted_iota(jnp.int32, (HALF, LANES), 1)
                 keys[d, half, LATENT:] = jnp.where(lane < ROPE, 0.0, 1.0).astype(bf16)
 
-    table_in.wait()
-    table_rows[...] = table[...].T
     kv_in.wait()
-    own_table = table_rows[pl.ds(pl.multiple_of(h * QTR, QTR), QTR), :]
-    own_cos, own_sin = own_table[:, :HALF_ROPE], own_table[:, HALF_ROPE:]
-    own_rope = kv[:, LATENT:].astype(f32)
-    low, high = own_rope[:, :HALF_ROPE], own_rope[:, HALF_ROPE:]
+    keys[0, quarter, :LATENT] = kv[:, :LATENT]
     seg_in.wait()
     place = lax.broadcasted_iota(jnp.int32, (QTR, ROPE), 0)
     ids = jnp.zeros((QTR, ROPE), jnp.int32)
     for j in range(QTR):
         ids = jnp.where(place == j, seg[j], ids)
     own_mark = jnp.where(lax.broadcasted_iota(jnp.int32, (QTR, ROPE), 1) == ids, 1.0, 0.0)
-    keys[0, quarter, :LATENT] = kv[:, :LATENT]
+    table_in.wait()
+    table_rows[...] = table[...].T
+    own_table = table_rows[pl.ds(pl.multiple_of(h * QTR, QTR), QTR), :]
+    own_cos, own_sin = own_table[:, :HALF_ROPE], own_table[:, HALF_ROPE:]
+    own_rope = kv[:, LATENT:].astype(f32)
+    low, high = own_rope[:, :HALF_ROPE], own_rope[:, HALF_ROPE:]
     keys[0, quarter, LATENT:] = jnp.concatenate(
         [low * own_cos - high * own_sin, low * own_sin + high * own_cos, own_mark], axis=1
     ).astype(bf16)

time: 45 us -> 45 us (level)
  no operation moved by 1% of the time
where the time goes in v2:
time: 45 us; the launch traced here: 44.9 us
  Pallas kernels  43 us (96%)
  local copies, waits for them, and re-layouts  1.88 us (4%)
    pallas_call x1, Pallas kernels, local(): pl.pallas_call(kernel, out_shape=jax.ShapeDtypeStruct((TOK, HEADS * VDIM)...  43 us
    unnamed x1, local copies, waits for them, and re-layouts  1.88 us

profile of v2, /device:TPU:35, one launch (start us, length us, event | category | flops | bytes accessed | tf_op | source)
XLA Modules:
  0.0 44.9 jit_solution(11097479557066046173)
XLA Ops:
  0.0 43.0 %latent_attention.1 = bf16[128,2048]{1,0:T(8,128)(2,1)} custom-call(f32[64,64,128]{2,1,0:T(8,128)} %constant.2.clone.table_hbm, bf16[16,576,128]{2,1,0:T(8,128)(2,1)} %bitcast.1, bf16[32,576]{1,0:T(8,128)(2,1)} %kv_hbm.1, s32[32]{0:T(128)} %seg_hbm.1, bf16[16,512,128]{2,1,0:T(8,128)(2,1)} %up_hbm.1), custom_call_target="tpu_custom_call" | custom-call | tf_op jit(solution)/shard_map/latent_attention/pallas_call | solution.py:338
  43.0 1.9 %copy.7 = bf16[128,2048]{1,0:T(8,128)(2,1)} copy(bf16[128,2048]{1,0:T(8,128)(2,1)} %latent_attention.1) | data formatting | bytes 1048576
